TPU v7x, 128 devices: a whole 4x4x4 slice. The times are simulated.
128 devices in a mesh: blk: 16 (over x, z_lo, core), uly: 8 (over z_hi, y).
Axes of the slice: x: 4, y: 4, z: 4 (z_hi: 2, z_lo: 2; z = z_hi * 2 + z_lo), core: 2. Of those that a mesh axis runs over, the one named last changes fastest.
Arguments:
- activations: bfloat16 [12288, 4096], P(('blk', 'uly')), may hold values from -64 to 64
- input_norm_gain: float32 [4096], replicated, may hold values from 0.5 to 2
- query_weight: bfloat16 [4096, 4096], P(None, 'uly'), may hold values from -3 to 3
- key_weight: bfloat16 [4096, 1024], P(None, 'uly'), may hold values from -3 to 3
- value_weight: bfloat16 [4096, 1024], P(None, 'uly'), may hold values from -0.09375 to 0.09375
- output_weight: bfloat16 [4096, 4096], P('uly'), may hold values from -1 to 1
- adapter_down_maps: bfloat16 [4096, 384], replicated, may hold values from -0.09375 to 0.09375
- query_up_maps: bfloat16 [128, 4096], P(None, 'uly'), may hold values from -0.375 to 0.375
- key_up_maps: bfloat16 [128, 1024], P(None, 'uly'), may hold values from -0.375 to 0.375
- value_up_maps: bfloat16 [128, 1024], P(None, 'uly'), may hold values from -0.375 to 0.375
- output_down_maps: bfloat16 [4096, 128], P('uly'), may hold values from -0.5 to 0.5
- output_up_maps: bfloat16 [128, 4096], replicated, may hold values from -1.5 to 1.5
- segment_index: int32 [12288], replicated, may hold values from 0 to 3, never falling along the last dimension, each value on 1 to 9216 neighbouring positions
- segment_adapter: int32 [4], replicated, may hold values from 0 to 7
Outputs:
- attn_out: bfloat16 [12288, 4096], P(('blk', 'uly'))
Inputs may be any that keep to these rules, and one draw needn't show every extreme that they name: `segment_index`: never falling along the sequence; each of the 4 segments covers 1 to 9216 tokens, and one covers exactly that many. `segment_adapter`: one adapter per segment; segments may share one.
All inputs are finite; a program needn't handle non-finite values.
Results may differ from a plain program's by a relative error of at most 0.019.
The roundings to bfloat16 on the way count: a program that leaves them out, or rounds other values in their place, can miss the bound.
Values may be sent and summed in bfloat16 or wider, within the bound.
No kernel may reach another device: no remote copies, remote signals or barrier semaphores. Data moves between devices by JAX's collectives and lax.ppermute only.
A program may use at most 192 MiB of HBM per device.

v0:
```python
import functools
import math

import jax
import jax.numpy as jnp
from jax import lax
from jax.experimental import pallas as pl
from jax.experimental.pallas import tpu as pltpu
from jax.sharding import PartitionSpec as P

HEAD_SIZE = 128
ADAPTER_RANK = 16
ADAPTER_COUNT = 8
GROUP = 4
PIECE = 96
HALF = 384
BLOCK = 768
BLOCKS = 16
OTHER = 2
EPS_NORM = 1e-05
ADAPTER_SCALE = 2.0
MASKED = -1e30
LEAST = -1e20
EXP2_SCALE = math.log2(math.e) / math.sqrt(HEAD_SIZE)
MIB = 2**20
HELD = pl.BlockSpec(memory_space=pltpu.VMEM)
UNIT = 48
CHUNKS = (0, 1, 2, 5, 6, 7, 8, 9, 3, 4, 10, 11, 12, 13, 14, 15)
HALF_CHUNKS = len(CHUNKS) // 2
HELD = pl.BlockSpec(memory_space=pltpu.VMEM)
WIDTH = 512

INFO = 26


def halves_of(pieces):
    return sum(((2 * p, 2 * p + 1) for p in pieces), ())


def pos_of(info, halves):
    index = lax.broadcasted_iota(jnp.int32, (UNIT * len(halves), 1), 0)
    pos = index
    for i, half in enumerate(halves):
        start = info[half // 2] + half % 2 * UNIT
        pos = jnp.where(index >= i * UNIT, index + (start - i * UNIT), pos)
    return pos


def start_of(info, pos):
    start = jnp.zeros_like(pos)
    for s in range(8, 11):
        start = jnp.where(pos >= info[s], info[s], start)
    return start


def tenant_of(info, pos):
    tenant = jnp.zeros_like(pos) + info[11]
    for s in range(3):
        tenant = jnp.where(pos >= info[8 + s], info[12 + s], tenant)
    return tenant


def keep_columns(info, halves, columns):
    tenant = tenant_of(info, pos_of(info, halves))
    column = lax.broadcasted_iota(jnp.int32, (len(halves) * UNIT, columns), 1)
    return (column // ADAPTER_RANK) % ADAPTER_COUNT == tenant


def project_kernel(info, *refs, halves, parts, targets, earlier):
    rows, refs = refs[:parts], refs[parts:]
    if earlier:
        before, refs = refs[0], refs[1:]
    down, weights, ups = refs[0], refs[1 : 1 + len(targets)], refs[1 + len(targets) : -2]
    out, acc = refs[-2:]
    step = pl.program_id(0)
    hidden = ADAPTER_COUNT * ADAPTER_RANK
    chunk = down.shape[0] // pl.num_programs(0)
    columns = pl.ds(pl.multiple_of(step * chunk, chunk), chunk)
    x = jnp.concatenate([r[:, columns] for r in rows], axis=0)
    w = [w[columns] for w in weights]
    w += [down[columns, t * hidden : (t + 1) * hidden] for t in targets]
    product = jnp.dot(x, jnp.concatenate(w, axis=1), preferred_element_type=jnp.float32)

    @pl.when(step == 0)
    def _():
        acc[...] = product

    @pl.when(step > 0)
    def _():
        acc[...] += product

    @pl.when(step == pl.num_programs(0) - 1)
    def _():
        keep = keep_columns(info, halves, hidden)
        new = 0
        if earlier:
            new = before.shape[0]
            out[:new] = before[...]
        at, low_at = 0, out.shape[1]
        for weight, up in zip(weights, ups):
            width = weight.shape[1]
            low = jnp.where(keep, acc[:, low_at : low_at + hidden], 0.0).astype(jnp.bfloat16)
            adapted = jnp.dot(low, up[...], preferred_element_type=jnp.float32)
            out[new:, at : at + width] = (
                acc[:, at : at + width] + ADAPTER_SCALE * adapted
            ).astype(jnp.bfloat16)
            at += width
            low_at += hidden


def project(info, rows, halves, down, targets, weights, ups, before=()):
    depth, count = down.shape[0], sum(r.shape[0] for r in rows)
    width = sum(w.shape[1] for w in weights)
    wide = width + ADAPTER_COUNT * ADAPTER_RANK * len(targets)
    return pl.pallas_call(
        functools.partial(
            project_kernel,
            halves=halves,
            parts=len(rows),
            targets=targets,
            earlier=bool(before),
        ),
        out_shape=jax.ShapeDtypeStruct((count + sum(b.shape[0] for b in before), width), jnp.bfloat16),
        grid_spec=pltpu.PrefetchScalarGridSpec(
            num_scalar_prefetch=1,
            grid=(depth // 1024,),
            in_specs=[HELD] * (len(rows) + len(before) + 1 + 2 * len(targets)),
            out_specs=HELD,
            scratch_shapes=[pltpu.VMEM((count, wide), jnp.float32)],
        ),
        compiler_params=pltpu.CompilerParams(vmem_limit_bytes=14 * MIB),
        cost_estimate=pl.CostEstimate(
            flops=4 * count * depth * wide,
            bytes_accessed=2 * depth * (wide + count),
            transcendentals=0,
        ),
    )(info, *rows, *before, down, *weights, *ups)


def positions(info, bases):
    tokens = len(bases) * PIECE
    column = lax.broadcasted_iota(jnp.int32, (1, GROUP * tokens), 1)
    pos = column
    for h in range(GROUP):
        for i, base in enumerate(bases):
            at = h * tokens + i * PIECE
            pos = jnp.where(column >= at, column + (info[base] - at), pos)
    return pos


def attend_kernel(info, q1, q2, *refs, sections, parts):
    shares, refs = refs[: len(parts)], refs[len(parts) :]
    if parts:
        out, kv, qt, acc, peak, held, held_peak = refs
    else:
        kv, out, qt, acc, peak, held, held_peak = refs
    for ref, (dx, dz, dc, at) in zip(shares, parts):
        x = lax.rem(info[23] + dx, 4)
        z = info[24] if dz == 0 else 1 - info[24]
        c = info[25] if dc == 0 else 1 - info[25]
        kv[x * 4 + z * 2 + c, at : at + ref.shape[0]] = ref[...]
    index = lax.broadcasted_iota(jnp.int32, (BLOCK, 1), 0)
    offsets = index
    for i, half in enumerate(CHUNKS):
        start = info[15 + half // 2] * PIECE + half % 2 * UNIT
        offsets = jnp.where(index >= i * UNIT, index + (start - i * UNIT), offsets)

    def of_block(t, at):
        here = lambda i: CHUNKS[i] < 8
        spans, i = [], 0
        while i < len(CHUNKS):
            n = 1
            while i + n < len(CHUNKS) and here(i + n) == here(i):
                n += 1
            device = t if here(i) else t ^ OTHER
            spans.append(kv[device, i * UNIT : (i + n) * UNIT, at : at + HEAD_SIZE])
            i += n
        return jnp.concatenate(spans, axis=0)

    done = 0
    for pieces in sections:
        tokens = len(pieces) * PIECE
        total = GROUP * tokens
        width = WIDTH if total % WIDTH == 0 else PIECE * GROUP
        rows = []
        for half in halves_of(pieces):
            place = CHUNKS.index(half)
            ref, place = (q1, place) if place < HALF_CHUNKS else (q2, place - HALF_CHUNKS)
            rows.append(ref[place * UNIT : (place + 1) * UNIT])
        q = jnp.concatenate(rows, axis=0)
        q = [q[:, h * HEAD_SIZE : (h + 1) * HEAD_SIZE] for h in range(GROUP)]
        qt[:, :total] = jnp.concatenate(q, axis=0).T
        acc[:, :total] = jnp.zeros((HEAD_SIZE + 8, total), jnp.float32)
        peak[:, :total] = jnp.full((1, total), LEAST, jnp.float32)
        pos = positions(info, pieces)
        low = start_of(info, pos)
        first = last = info[pieces[0]]
        for piece in pieces[1:]:
            first, last = jnp.minimum(first, info[piece]), jnp.maximum(last, info[piece])
        last = last + (PIECE - 1)
        n0 = start_of(info, first) // BLOCK
        own = first // BLOCK
        m1 = jnp.clip((start_of(info, last) + BLOCK - 1) // BLOCK, n0, own)

        def step(now, later, causal=False, starts=False):
            if later is not None:
                keys = of_block(later, 0)
            if now is not None:
                values = jnp.concatenate(
                    [of_block(now, HEAD_SIZE).T, jnp.ones((8, BLOCK), jnp.bfloat16)], axis=0
                )
            for c in range(0, total, width):
                at = slice(c, c + width)
                if now is not None:
                    old = peak[:, at]
                    fresh = jnp.maximum(old, held_peak[:, at])
                    weights = jnp.exp2((held[:, at] - fresh) * EXP2_SCALE).astype(jnp.bfloat16)
                    decay = jnp.exp2((old - fresh) * EXP2_SCALE)
                    peak[:, at] = fresh
                if later is not None:
                    scores = jnp.dot(keys, qt[:, at], preferred_element_type=jnp.float32)
                    if causal or starts:
                        key_pos = offsets + later * BLOCK
                        allowed = key_pos >= low[:, at]
                        if causal:
                            allowed &= key_pos <= pos[:, at]
                        scores = jnp.where(allowed, scores, MASKED)
                    held[:, at] = scores
                    held_peak[:, at] = jnp.max(scores, axis=0, keepdims=True)
                if now is not None:
                    acc[:, at] = acc[:, at] * decay + jnp.dot(
                        values, weights, preferred_element_type=jnp.float32
                    )

        def starting_step(j, now):
            step(now, j, starts=True)
            return j

        def plain_step(j, now):
            step(now, j)
            return j

        step(None, own, causal=True)
        now = lax.fori_loop(n0, m1, starting_step, own)
        now = lax.fori_loop(m1, own, plain_step, now)
        step(now, None)
        mixed = acc[:HEAD_SIZE, :total] / acc[HEAD_SIZE : HEAD_SIZE + 1, :total]
        mixed = mixed.T.astype(jnp.bfloat16)
        for h in range(GROUP):
            out[done : done + tokens, h * HEAD_SIZE : (h + 1) * HEAD_SIZE] = mixed[
                h * tokens : (h + 1) * tokens
            ]
        done += tokens


def attend(info, queries, sections, shares=(), kv=None):
    parts = [k[:4] for k in shares]
    arrays = [k[4] for k in shares] if kv is None else [kv]
    tokens = [len(s) * PIECE for s in sections]
    total = GROUP * max(tokens)
    out_shape = jax.ShapeDtypeStruct((sum(tokens), GROUP * HEAD_SIZE), jnp.bfloat16)
    out_specs = pl.BlockSpec(out_shape.shape, lambda i, s: (0, 0))
    if kv is None:
        out_shape = (out_shape, jax.ShapeDtypeStruct((BLOCKS, BLOCK, 2 * HEAD_SIZE), jnp.bfloat16))
        out_specs = (out_specs, HELD)
    return pl.pallas_call(
        functools.partial(attend_kernel, sections=sections, parts=parts),
        out_shape=out_shape,
        grid_spec=pltpu.PrefetchScalarGridSpec(
            num_scalar_prefetch=1,
            grid=(1,),
            in_specs=[HELD] * (2 + len(arrays)),
            out_specs=out_specs,
            scratch_shapes=[
                pltpu.VMEM((HEAD_SIZE, total), jnp.bfloat16),
                pltpu.VMEM((HEAD_SIZE + 8, total), jnp.float32),
                pltpu.VMEM((1, total), jnp.float32),
                pltpu.VMEM((BLOCK, total), jnp.float32),
                pltpu.VMEM((1, total), jnp.float32),
            ],
        ),
        compiler_params=pltpu.CompilerParams(vmem_limit_bytes=20 * MIB),
        cost_estimate=pl.CostEstimate(
            flops=4 * GROUP * sum(tokens) * BLOCKS * BLOCK * HEAD_SIZE,
            bytes_accessed=8 * MIB,
            transcendentals=GROUP * sum(tokens) * BLOCKS * BLOCK,
        ),
    )(info, *queries, *arrays)


def output_kernel(info, mixed, weight, down, up, *rest, bases):
    *outs, rows = rest
    depth = mixed.shape[1]

    @pl.when(pl.program_id(0) == 0)
    def _():
        lows = jnp.dot(mixed[...], down[...], preferred_element_type=jnp.float32)
        lows = jnp.where(keep_columns(info, halves_of(bases), lows.shape[1]), ADAPTER_SCALE * lows, 0.0)
        rows[:, :depth] = mixed[...]
        rows[:, depth:] = lows.astype(jnp.bfloat16)

    chunk = up.shape[1] // pl.num_programs(0)
    columns = pl.ds(pl.multiple_of(pl.program_id(0) * chunk, chunk), chunk)
    weights = jnp.concatenate([weight[:, columns], up[:, columns]], axis=0)
    result = jnp.dot(rows[...], weights, preferred_element_type=jnp.float32).astype(jnp.bfloat16)
    at = 0
    for out in outs:
        out[:, columns] = result[at : at + out.shape[0]]
        at += out.shape[0]


def output(info, mixed, weight, down, up, bases, halved):
    rows = sum(((PIECE // 2,) * 2 if b in halved else (PIECE,) for b in bases), ())
    features = weight.shape[1]
    chunk = 1024
    depth = weight.shape[0] + up.shape[0]
    return pl.pallas_call(
        functools.partial(output_kernel, bases=bases),
        out_shape=tuple(jax.ShapeDtypeStruct((n, features), jnp.bfloat16) for n in rows),
        grid_spec=pltpu.PrefetchScalarGridSpec(
            num_scalar_prefetch=1,
            grid=(features // chunk,),
            in_specs=[HELD] * 4,
            out_specs=(HELD,) * len(rows),
            scratch_shapes=[pltpu.VMEM((mixed.shape[0], depth), jnp.bfloat16)],
        ),
        compiler_params=pltpu.CompilerParams(vmem_limit_bytes=12 * MIB),
        cost_estimate=pl.CostEstimate(
            flops=2 * mixed.shape[0] * depth * features,
            bytes_accessed=2 * features * (depth + mixed.shape[0]),
            transcendentals=0,
        ),
    )(info, mixed, weight, down, up)


def normalize_kernel(activations, gain, out, top, end):
    half = top.shape[0]
    step = pl.program_id(0)
    values = activations[...].astype(jnp.float32)
    power = jnp.mean(values * values, axis=1, keepdims=True)
    normed = (values * lax.rsqrt(power + EPS_NORM) * gain[...]).astype(jnp.bfloat16)
    out[pl.ds(pl.multiple_of(step * half, half), half)] = normed

    @pl.when(step == 0)
    def _():
        top[...] = normed

    @pl.when(step == 1)
    def _():
        end[...] = normed


def normalize(activations, input_norm_gain):
    rows, features = activations.shape
    half = rows // 2
    shape = lambda n: jax.ShapeDtypeStruct((n, features), jnp.bfloat16)
    return pl.pallas_call(
        normalize_kernel,
        out_shape=(shape(rows), shape(half), shape(half)),
        grid=(2,),
        in_specs=[
            pl.BlockSpec((half, features), lambda i: (i, 0)),
            pl.BlockSpec((1, features), lambda i: (0, 0)),
        ],
        out_specs=(HELD,) * 3,
        compiler_params=pltpu.CompilerParams(vmem_limit_bytes=58 * MIB),
    )(activations, input_norm_gain[None, :])


def along_y(rows, hop):
    return lax.ppermute(
        rows, "uly", [(z * 4 + y, z * 4 + (y + hop) % 4) for z in range(2) for y in range(4)]
    )


def across_z(rows):
    pairs = [(b * 8 + u, (b ^ OTHER) * 8 + (u ^ 4)) for b in range(16) for u in range(8)]
    return lax.ppermute(rows, ("blk", "uly"), pairs)


def flipped(rows, bit):
    return lax.ppermute(rows, "blk", [(b, b ^ bit) for b in range(16)])


def along_x(rows, hop):
    return lax.ppermute(rows, "blk", [(b, (b + 4 * hop) % 16) for b in range(16)])


def in_steps(kv, other, from_m, from_p, far):
    other_m, other_p, other_far = along_x(other, 1), along_x(other, -1), flipped(far, 2)
    return [
        (0, 0, 0, kv),
        (3, 0, 0, from_m),
        (1, 0, 0, from_p),
        (2, 0, 0, far),
        (0, 1, 0, other),
        (3, 1, 0, other_m),
        (1, 1, 0, other_p),
        (2, 1, 0, other_far),
    ]


def both_cores(found):
    return [(dx, dz, 0, at, a) for dx, dz, at, a in found] + [
        (dx, dz, 1, at, flipped(a, 1)) for dx, dz, at, a in found
    ]


def plan(segment_index, segment_adapter):
    block, head = lax.axis_index("blk"), lax.axis_index("uly")
    z, y = head // 4, head % 4
    ys = [y, (y + 3) % 4, (y + 1) % 4, (y + 2) % 4]
    here = [z * 4 + p for p in ys]
    there = [(1 - z) * 4 + p for p in ys]
    firsts = [block * BLOCK + p * PIECE for p in here]
    firsts += [(block ^ OTHER) * BLOCK + p * PIECE for p in there]
    ends = jnp.sum(
        segment_index[None, :] < jnp.arange(1, 4, dtype=jnp.int32)[:, None], axis=1, dtype=jnp.int32
    )
    return jnp.concatenate(
        [
            jnp.stack(firsts).astype(jnp.int32),
            ends,
            segment_adapter,
            jnp.stack(here + there).astype(jnp.int32),
            jnp.stack([block // 4, (block // 2) % 2, block % 2]).astype(jnp.int32),
        ]
    )


def added(*terms):
    return sum(t.astype(jnp.float32) for t in terms).astype(jnp.bfloat16)


def shards(
    activations,
    input_norm_gain,
    query_weight,
    key_weight,
    value_weight,
    output_weight,
    adapter_down_maps,
    query_up_maps,
    key_up_maps,
    value_up_maps,
    output_down_maps,
    output_up_maps,
    segment_index,
    segment_adapter,
):
    info = plan(segment_index, segment_adapter)
    mid = PIECE // 2
    own, own_top, own_end = normalize(activations, input_norm_gain)
    m_top, p_end, other = along_y(own_top, 1), along_y(own_end, -1), across_z(own)
    own_top, own_end, other = lax.optimization_barrier((own_top, own_end, other))
    m_end, p_top = along_y(own_end, 1), along_y(own_top, -1)
    far_top, far_end = along_y(m_top, 1), along_y(p_end, -1)
    other_m, other_p = along_y(other, 1), along_y(other, -1)
    other_far = across_z(jnp.concatenate([far_top, far_end], axis=0))

    down = adapter_down_maps
    kv_weights, kv_ups = (key_weight, value_weight), (key_up_maps, value_up_maps)
    rows1 = [own, m_top, p_end, far_top, far_end, other]
    rows2 = [m_end, p_top, other_m, other_p, other_far]
    kv = project(info, rows1, CHUNKS[:HALF_CHUNKS], down, (1, 2), kv_weights, kv_ups)
    q_operands = (down, (0,), (query_weight,), (query_up_maps,))
    q1 = project(info, rows1, CHUNKS[:HALF_CHUNKS], *q_operands)
    kv, q1 = lax.optimization_barrier((kv, q1))
    kv = project(info, rows2, CHUNKS[HALF_CHUNKS:], down, (1, 2), kv_weights, kv_ups, before=(kv,))
    steps = flipped(kv, 2), along_x(kv, 1), along_x(kv, -1), along_x(kv, 2)
    q2 = project(info, rows2, CHUNKS[HALF_CHUNKS:], *q_operands)
    other, q2 = lax.optimization_barrier((steps[0], q2))
    steps = (other, *steps[1:])
    shares = both_cores(in_steps(kv, *steps))
    queries = (q1, q2)

    def products(mixed, bases, halved=()):
        weights = output_weight, output_down_maps, output_up_maps
        return output(info, mixed, *weights, bases, halved)

    mixed, kv = attend(info, queries, ((7, 5, 6),), shares)
    bf, bm, bp = products(mixed, (7, 5, 6))
    for_far, from_m, from_p = across_z(bf), along_y(bp, 1), along_y(bm, -1)
    mixed = attend(info, queries, ((3, 1, 2), (4,)), kv=kv)
    af, am_top, am_end, ap_top, ap_end, b0 = products(mixed, (3, 1, 2, 4), halved=(1, 2))
    from_m_end, from_p_top = along_y(ap_end, 1), along_y(am_top, -1)
    far = added(af, for_far)
    other_sum = added(b0, from_m, from_p)
    queries, far, other_sum = lax.optimization_barrier((queries, far, other_sum))
    top, end = along_y(far[:mid], 1), along_y(far[mid:], -1)
    for_own = across_z(other_sum)
    to_p, to_m = added(ap_top, top), added(am_end, end)
    from_m_top, from_p_end = along_y(to_p, 1), along_y(to_m, -1)
    (a0,) = products(attend(info, queries, ((0,),), kv=kv), (0,))
    late = jnp.concatenate([from_m_top, from_p_end], axis=0)
    early = jnp.concatenate([from_p_top, from_m_end], axis=0)
    return added(late, early, for_own, a0)


def solution(mesh):
    return jax.shard_map(
        shards,
        mesh=mesh,
        in_specs=(
            P(("blk", "uly"), None),
            P(),
            P(None, "uly"),
            P(None, "uly"),
            P(None, "uly"),
            P("uly", None),
            P(),
            P(None, "uly"),
            P(None, "uly"),
            P(None, "uly"),
            P("uly", None),
            P(),
            P(),
            P(),
        ),
        out_specs=P(("blk", "uly"), None),
        check_vma=False,
    )
```

profile of v0, /device:TPU:6, one launch (start us, length us, event | category | flops | bytes accessed | tf_op | source)
XLA Modules:
  0.0 170.5 jit_solution(8592445031052205343)
XLA Ops:
  2.8 4.0 %collective-permute-start.4 = (bf16[96,4096]{1,0:T(8,128)(2,1)}, bf16[96,4096]{1,0:T(8,128)(2,1)}, u32[]{:S(2)}, u32[]{:S(2)}) collective-permute-start(bf16[96,4096]{1,0:T(8,128)(2,1)} %get-tuple-element.30.refs_0_), channel_id=1, source_target_pairs={{0,20},{1,21},{2,22},{3,23},{4,16},{5,17},{6,18},{7,19},{8,28},{9,... | collective-permute-start | bytes 2359304 | tf_op jit(solution)/shard_map/ppermute | solution.py:378
  10.1 8.8 %collective-permute-done.refs_1_ = bf16[48,4096]{1,0:T(8,128)(2,1)S(1)} collective-permute-done((bf16[48,4096]{1,0:T(8,128)(2,1)}, bf16[48,4096]{1,0:T(8,128)(2,1)S(1)}, u32[]{:S(2)}, u32[]{:S(2)}) %collective-permute-start) | collective-permute-done | bytes 393248 | tf_op jit(solution)/shard_map/ppermute | solution.py:371
  24.7 3.0 %collective-permute-start.8 = (bf16[96,4096]{1,0:T(8,128)(2,1)}, bf16[96,4096]{1,0:T(8,128)(2,1)}, u32[]{:S(2)}, u32[]{:S(2)}) collective-permute-start(bf16[96,4096]{1,0:T(8,128)(2,1)} %collective-permute-done.4.refs_5_), channel_id=1, source_target_pairs={{0,3},{1,0},{2,1},{3,2},{4,7},{5,4},{6,5},{7,6},{8,11},{9,8},{10,9... | collective-permute-start | bytes 2359304 | tf_op jit(solution)/shard_map/ppermute | solution.py:371
  39.7 4.7 %shard_map.137.refs_5_ = bf16[384,256]{1,0:T(8,128)(2,1)S(1)} custom-call(s32[26]{0:T(128)S(1)} %concatenate.12.info, bf16[96,4096]{1,0:T(8,128)(2,1)S(1)} %copy-done.8, bf16[48,4096]{1,0:T(8,128)(2,1)S(1)} %collective-permute-done.refs_1_, bf16[48,4096]{1,0:T(8,128)(2,1)} %collective-permute-done.1.refs_2_, ...), custom_call_target="tpu_custom_call" | custom-call | flops 3221225472 | bytes 7340032 | tf_op jit(solution)/shard_map/pallas_call | solution.py:115
  44.5 5.9 %shard_map.138.q1 = bf16[384,512]{1,0:T(8,128)(2,1)S(1)} custom-call(s32[26]{0:T(128)S(1)} %concatenate.12.info, bf16[96,4096]{1,0:T(8,128)(2,1)S(1)} %copy-done.8, bf16[48,4096]{1,0:T(8,128)(2,1)S(1)} %collective-permute-done.refs_1_, bf16[48,4096]{1,0:T(8,128)(2,1)} %collective-permute-done.1.refs_2_, bf16[48,4096]{1,0:T(8,128)(2,1)S(1)} %collective-permute-done.2.refs_3_, ...), custom_call_target="tpu_custom_call" | custom-call | flops 4026531840 | bytes 8388608 | tf_op jit(solution)/shard_map/pallas_call | solution.py:115
  50.3 5.7 %collective-permute-done.5.refs_0_ = bf16[48,4096]{1,0:T(8,128)(2,1)S(1)} collective-permute-done((bf16[48,4096]{1,0:T(8,128)(2,1)}, bf16[48,4096]{1,0:T(8,128)(2,1)S(1)}, u32[]{:S(2)}, u32[]{:S(2)}) %collective-permute-start.5) | collective-permute-done | bytes 393248 | tf_op jit(solution)/shard_map/ppermute | solution.py:371
  56.1 5.1 %shard_map.139.refs_0_ = bf16[768,256]{1,0:T(8,128)(2,1)S(1)} custom-call(s32[26]{0:T(128)S(1)} %concatenate.12.info, bf16[48,4096]{1,0:T(8,128)(2,1)S(1)} %collective-permute-done.5.refs_0_, bf16[48,4096]{1,0:T(8,128)(2,1)S(1)} %collective-permute-done.6.refs_1_, bf16[96,4096]{1,0:T(8,128)(2,1)} %collective-permute-done.7.refs_2_, ...), custom_call_target="tpu_custom_call" | custom-call | flops 3221225472 | bytes 7340032 | tf_op jit(solution)/shard_map/pallas_call | solution.py:115
  62.7 3.2 %collective-permute-start.11 = (bf16[768,256]{1,0:T(8,128)(2,1)S(1)}, bf16[768,256]{1,0:T(8,128)(2,1)S(1)}, u32[]{:S(2)}, u32[]{:S(2)}) collective-permute-start(bf16[768,256]{1,0:T(8,128)(2,1)S(1)} %shard_map.139.refs_0_), channel_id=1, source_target_pairs={{0,32},{8,40},{16,48},{24,56},{32,64},{40,72},{48,80},{56,88},{64,... | collective-permute-start | bytes 1179656 | tf_op jit(solution)/shard_map/ppermute | solution.py:386
  66.0 5.9 %shard_map.140.q2 = bf16[384,512]{1,0:T(8,128)(2,1)S(1)} custom-call(s32[26]{0:T(128)S(1)} %concatenate.12.info, bf16[48,4096]{1,0:T(8,128)(2,1)S(1)} %collective-permute-done.5.refs_0_, bf16[48,4096]{1,0:T(8,128)(2,1)S(1)} %collective-permute-done.6.refs_1_, bf16[96,4096]{1,0:T(8,128)(2,1)} %collective-permute-done.7.refs_2_, ...), custom_call_target="tpu_custom_call" | custom-call | flops 4026531840 | bytes 8388608 | tf_op jit(solution)/shard_map/pallas_call | solution.py:115
  76.8 3.5 %collective-permute-done.12.refs_2_ = bf16[768,256]{1,0:T(8,128)(2,1)S(1)} collective-permute-done((bf16[768,256]{1,0:T(8,128)(2,1)S(1)}, bf16[768,256]{1,0:T(8,128)(2,1)S(1)}, u32[]{:S(2)}, u32[]{:S(2)}) %collective-permute-start.12) | collective-permute-done | bytes 393248 | tf_op jit(solution)/shard_map/ppermute | solution.py:386
  80.4 3.2 %collective-permute-start.14 = (bf16[768,256]{1,0:T(8,128)(2,1)S(1)}, bf16[768,256]{1,0:T(8,128)(2,1)S(1)}, u32[]{:S(2)}, u32[]{:S(2)}) collective-permute-start(bf16[768,256]{1,0:T(8,128)(2,1)S(1)} %collective-permute-done.10.refs_4_), channel_id=1, source_target_pairs={{0,32},{8,40},{16,48},{24,56},{32,64},{40,72},{48,80},{56,88},{64,... | collective-permute-start | bytes 1179656 | tf_op jit(solution)/shard_map/ppermute | solution.py:386
  83.6 3.0 %collective-permute-done.16.refs_7_ = bf16[768,256]{1,0:T(8,128)(2,1)S(1)} collective-permute-done((bf16[768,256]{1,0:T(8,128)(2,1)S(1)}, bf16[768,256]{1,0:T(8,128)(2,1)S(1)}, u32[]{:S(2)}, u32[]{:S(2)}) %collective-permute-start.16) | collective-permute-done | bytes 393248 | tf_op jit(solution)/shard_map/ppermute | solution.py:382
  87.1 6.0 %collective-permute-done.15.refs_6_ = bf16[768,256]{1,0:T(8,128)(2,1)S(1)} collective-permute-done((bf16[768,256]{1,0:T(8,128)(2,1)S(1)}, bf16[768,256]{1,0:T(8,128)(2,1)S(1)}, u32[]{:S(2)}, u32[]{:S(2)}) %collective-permute-start.15) | collective-permute-done | bytes 393248 | tf_op jit(solution)/shard_map/ppermute | solution.py:386
  95.4 12.7 %shard_map.141 = (bf16[288,512]{1,0:T(8,128)(2,1)S(1)}, bf16[16,768,256]{2,1,0:T(8,128)(2,1)S(1)}) custom-call(s32[26]{0:T(128)S(1)} %concatenate.12.info, bf16[384,512]{1,0:T(8,128)(2,1)S(1)} %shard_map.138.q1, bf16[384,512]{1,0:T(8,128)(2,1)S(1)} %shard_map.140.q2, bf16[768,256]{1,0:T(8,128)(2,1)S(1)} %shard_map.139.refs_0_, ...), custom_call_target="tpu_custom_call" | custom-call | flops 7247757312 | bytes 8388608 | tf_op jit(solution)/shard_map/pallas_call | solution.py:266
  108.1 3.4 %shard_map.144 = (bf16[96,4096]{1,0:T(8,128)(2,1)S(1)}, bf16[96,4096]{1,0:T(8,128)(2,1)S(1)}, bf16[96,4096]{1,0:T(8,128)(2,1)S(1)}) custom-call(s32[26]{0:T(128)S(1)} %concatenate.12.info, bf16[288,512]{1,0:T(8,128)(2,1)S(1)} %get-tuple-element.43.mixed, bf16[512,4096]{1,0:T(8,128)(2,1)S(1)} %copy-done, bf16[512,128]{1,0:T(8,128)(2,1)S(1)} %copy-done.2, ...), custom_call_target="tpu_custom_call" | custom-call | flops 1509949440 | bytes 7602176 | tf_op jit(solution)/shard_map/pallas_call | solution.py:317
  111.9 3.2 %collective-permute-start.27 = (bf16[96,4096]{1,0:T(8,128)(2,1)S(1)}, bf16[96,4096]{1,0:T(8,128)(2,1)S(1)}, u32[]{:S(2)}, u32[]{:S(2)}) collective-permute-start(bf16[96,4096]{1,0:T(8,128)(2,1)S(1)} %get-tuple-element.47), channel_id=1, source_target_pairs={{0,3},{1,0},{2,1},{3,2},{4,7},{5,4},{6,5},{7,6},{8,11},{9,8},{10,9... | collective-permute-start | bytes 2359304 | tf_op jit(solution)/shard_map/ppermute | solution.py:371
  115.2 15.4 %shard_map.142.mixed = bf16[384,512]{1,0:T(8,128)(2,1)S(1)} custom-call(s32[26]{0:T(128)S(1)} %concatenate.12.info, bf16[384,512]{1,0:T(8,128)(2,1)S(1)} %shard_map.138.q1, bf16[384,512]{1,0:T(8,128)(2,1)S(1)} %shard_map.140.q2, bf16[16,768,256]{2,1,0:T(8,128)(2,1)S(1)} %get-tuple-element.40.refs_0_), custom_call_target="tpu_custom_call" | custom-call | flops 9663676416 | bytes 8388608 | tf_op jit(solution)/shard_map/pallas_call | solution.py:266
  130.6 4.0 %shard_map.143 = (bf16[96,4096]{1,0:T(8,128)(2,1)S(1)}, bf16[48,4096]{1,0:T(8,128)(2,1)S(1)}, bf16[48,4096]{1,0:T(8,128)(2,1)S(1)}, bf16[48,4096]{1,0:T(8,128)(2...) custom-call(s32[26]{0:T(128)S(1)} %concatenate.12.info, bf16[384,512]{1,0:T(8,128)(2,1)S(1)} %shard_map.142.mixed, ...), custom_call_target="tpu_custom_call" | custom-call | flops 2013265920 | bytes 8388608 | tf_op jit(solution)/shard_map/pallas_call | solution.py:317
  135.5 3.2 %collective-permute-start.32 = (bf16[48,4096]{1,0:T(8,128)(2,1)S(1)}, bf16[48,4096]{1,0:T(8,128)(2,1)S(1)}, u32[]{:S(2)}, u32[]{:S(2)}) collective-permute-start(bf16[48,4096]{1,0:T(8,128)(2,1)S(1)} %get-tuple-element.50), channel_id=1, source_target_pairs={{0,3},{1,0},{2,1},{3,2},{4,7},{5,4},{6,5},{7,6},{8,11},{9,8},{10,9... | collective-permute-start | bytes 1179656 | tf_op jit(solution)/shard_map/ppermute | solution.py:371
  138.7 3.2 %collective-permute-start.30 = (bf16[48,4096]{1,0:T(8,128)(2,1)S(1)}, bf16[48,4096]{1,0:T(8,128)(2,1)S(1)}, u32[]{:S(2)}, u32[]{:S(2)}) collective-permute-start(bf16[48,4096]{1,0:T(8,128)(2,1)S(1)} %get-tuple-element.56), channel_id=1, source_target_pairs={{0,3},{1,0},{2,1},{3,2},{4,7},{5,4},{6,5},{7,6},{8,11},{9,8},{10,9... | collective-permute-start | bytes 1179656 | tf_op jit(solution)/shard_map/ppermute | solution.py:371
  141.9 4.0 %collective-permute-start.34 = (bf16[96,4096]{1,0:T(8,128)(2,1)S(1)}, bf16[96,4096]{1,0:T(8,128)(2,1)S(1)}, u32[]{:S(2)}, u32[]{:S(2)}) collective-permute-start(bf16[96,4096]{1,0:T(8,128)(2,1)S(1)} %add_convert_fusion.1), channel_id=1, source_target_pairs={{0,20},{1,21},{2,22},{3,23},{4,16},{5,17},{6,18},{7,19},{8,28},{9,... | collective-permute-start | bytes 2359304 | tf_op jit(solution)/shard_map/ppermute | solution.py:378
  148.0 8.1 %collective-permute-done.30 = bf16[48,4096]{1,0:T(8,128)(2,1)S(1)} collective-permute-done((bf16[48,4096]{1,0:T(8,128)(2,1)S(1)}, bf16[48,4096]{1,0:T(8,128)(2,1)S(1)}, u32[]{:S(2)}, u32[]{:S(2)}) %collective-permute-start.30) | collective-permute-done | bytes 393248 | tf_op jit(solution)/shard_map/ppermute | solution.py:371
  156.2 3.8 %collective-permute-start.31 = (bf16[48,4096]{1,0:T(8,128)(2,1)S(1)}, bf16[48,4096]{1,0:T(8,128)(2,1)S(1)}, u32[]{:S(2)}, u32[]{:S(2)}) collective-permute-start(bf16[48,4096]{1,0:T(8,128)(2,1)S(1)} %add_convert_fusion.3), channel_id=1, source_target_pairs={{0,3},{1,0},{2,1},{3,2},{4,7},{5,4},{6,5},{7,6},{8,11},{9,8},{10,9... | collective-permute-start | bytes 1179656 | tf_op jit(solution)/shard_map/ppermute | solution.py:371
  160.0 5.0 %shard_map.145.mixed = bf16[96,512]{1,0:T(8,128)(2,1)S(1)} custom-call(s32[26]{0:T(128)S(1)} %concatenate.12.info, bf16[384,512]{1,0:T(8,128)(2,1)S(1)} %shard_map.138.q1, bf16[384,512]{1,0:T(8,128)(2,1)S(1)} %shard_map.140.q2, bf16[16,768,256]{2,1,0:T(8,128)(2,1)S(1)} %get-tuple-element.40.refs_0_), custom_call_target="tpu_custom_call" | custom-call | flops 2415919104 | bytes 8388608 | tf_op jit(solution)/shard_map/pallas_call | solution.py:266
  (95 shorter events, 42.0 us)
Async XLA Ops:
  2.8 21.9 %collective-permute-start.4 = (bf16[96,4096]{1,0:T(8,128)(2,1)}, bf16[96,4096]{1,0:T(8,128)(2,1)}, u32[]{:S(2)}, u32[]{:S(2)}) collective-permute-start(bf16[96,4096]{1,0:T(8,128)(2,1)} %get-tuple-element.30.refs_0_), channel_id=1, source_target_pairs={{0,20},{1,21},{2,22},{3,23},{4,16},{5,17},{6,18},{7,19},{8,28},{9,... | collective-permute-start | bytes 2359304 | tf_op jit(solution)/shard_map/ppermute | solution.py:378
  6.9 12.1 %collective-permute-start = (bf16[48,4096]{1,0:T(8,128)(2,1)}, bf16[48,4096]{1,0:T(8,128)(2,1)S(1)}, u32[]{:S(2)}, u32[]{:S(2)}) collective-permute-start(bf16[48,4096]{1,0:T(8,128)(2,1)} %get-tuple-element.36), channel_id=1, source_target_pairs={{0,1},{1,2},{2,3},{3,0},{4,5},{5,6},{6,7},{7,4},{8,9},{9,10},{10,1... | collective-permute-start | bytes 1179656 | tf_op jit(solution)/shard_map/ppermute | solution.py:371
  19.2 12.4 %collective-permute-start.3 = (bf16[48,4096]{1,0:T(8,128)(2,1)}, bf16[48,4096]{1,0:T(8,128)(2,1)S(1)}, u32[]{:S(2)}, u32[]{:S(2)}) collective-permute-start(bf16[48,4096]{1,0:T(8,128)(2,1)} %collective-permute-done.1.refs_2_), channel_id=1, source_target_pairs={{0,3},{1,0},{2,1},{3,2},{4,7},{5,4},{6,5},{7,6},{8,11},{9,8},{10,9... | collective-permute-start | bytes 1179656 | tf_op jit(solution)/shard_map/ppermute | solution.py:371
  24.7 31.3 %collective-permute-start.8 = (bf16[96,4096]{1,0:T(8,128)(2,1)}, bf16[96,4096]{1,0:T(8,128)(2,1)}, u32[]{:S(2)}, u32[]{:S(2)}) collective-permute-start(bf16[96,4096]{1,0:T(8,128)(2,1)} %collective-permute-done.4.refs_5_), channel_id=1, source_target_pairs={{0,3},{1,0},{2,1},{3,2},{4,7},{5,4},{6,5},{7,6},{8,11},{9,8},{10,9... | collective-permute-start | bytes 2359304 | tf_op jit(solution)/shard_map/ppermute | solution.py:371
  27.7 28.3 %collective-permute-start.7 = (bf16[96,4096]{1,0:T(8,128)(2,1)}, bf16[96,4096]{1,0:T(8,128)(2,1)}, u32[]{:S(2)}, u32[]{:S(2)}) collective-permute-start(bf16[96,4096]{1,0:T(8,128)(2,1)} %collective-permute-done.4.refs_5_), channel_id=1, source_target_pairs={{0,1},{1,2},{2,3},{3,0},{4,5},{5,6},{6,7},{7,4},{8,9},{9,10},{10,1... | collective-permute-start | bytes 2359304 | tf_op jit(solution)/shard_map/ppermute | solution.py:371
  32.5 23.5 %collective-permute-start.9 = (bf16[96,4096]{1,0:T(8,128)(2,1)}, bf16[96,4096]{1,0:T(8,128)(2,1)}, u32[]{:S(2)}, u32[]{:S(2)}) collective-permute-start(bf16[96,4096]{1,0:T(8,128)(2,1)} %pad_maximum_fusion), channel_id=1, source_target_pairs={{0,20},{1,21},{2,22},{3,23},{4,16},{5,17},{6,18},{7,19},{8,28},{9,... | collective-permute-start | bytes 2359304 | tf_op jit(solution)/shard_map/ppermute | solution.py:378
  33.0 23.1 %collective-permute-start.5 = (bf16[48,4096]{1,0:T(8,128)(2,1)}, bf16[48,4096]{1,0:T(8,128)(2,1)S(1)}, u32[]{:S(2)}, u32[]{:S(2)}) collective-permute-start(bf16[48,4096]{1,0:T(8,128)(2,1)} %get-tuple-element.35), channel_id=1, source_target_pairs={{0,1},{1,2},{2,3},{3,0},{4,5},{5,6},{6,7},{7,4},{8,9},{9,10},{10,1... | collective-permute-start | bytes 1179656 | tf_op jit(solution)/shard_map/ppermute | solution.py:371
  34.0 22.0 %collective-permute-start.6 = (bf16[48,4096]{1,0:T(8,128)(2,1)}, bf16[48,4096]{1,0:T(8,128)(2,1)S(1)}, u32[]{:S(2)}, u32[]{:S(2)}) collective-permute-start(bf16[48,4096]{1,0:T(8,128)(2,1)} %get-tuple-element.36), channel_id=1, source_target_pairs={{0,3},{1,0},{2,1},{3,2},{4,7},{5,4},{6,5},{7,6},{8,11},{9,8},{10,9... | collective-permute-start | bytes 1179656 | tf_op jit(solution)/shard_map/ppermute | solution.py:371
  61.2 13.6 %collective-permute-start.13 = (bf16[768,256]{1,0:T(8,128)(2,1)S(1)}, bf16[768,256]{1,0:T(8,128)(2,1)S(1)}, u32[]{:S(2)}, u32[]{:S(2)}) collective-permute-start(bf16[768,256]{1,0:T(8,128)(2,1)S(1)} %shard_map.139.refs_0_), channel_id=1, source_target_pairs={{0,64},{8,72},{16,80},{24,88},{32,96},{40,104},{48,112},{56,120},{... | collective-permute-start | bytes 1179656 | tf_op jit(solution)/shard_map/ppermute | solution.py:386
  62.7 17.6 %collective-permute-start.12 = (bf16[768,256]{1,0:T(8,128)(2,1)S(1)}, bf16[768,256]{1,0:T(8,128)(2,1)S(1)}, u32[]{:S(2)}, u32[]{:S(2)}) collective-permute-start(bf16[768,256]{1,0:T(8,128)(2,1)S(1)} %shard_map.139.refs_0_), channel_id=1, source_target_pairs={{0,96},{8,104},{16,112},{24,120},{32,0},{40,8},{48,16},{56,24},{64... | collective-permute-start | bytes 1179656 | tf_op jit(solution)/shard_map/ppermute | solution.py:386
  62.7 17.6 %collective-permute-start.17 = (bf16[768,256]{1,0:T(8,128)(2,1)S(1)}, bf16[768,256]{1,0:T(8,128)(2,1)S(1)}, u32[]{:S(2)}, u32[]{:S(2)}) collective-permute-start(bf16[768,256]{1,0:T(8,128)(2,1)S(1)} %shard_map.139.refs_0_), channel_id=1, source_target_pairs={{0,8},{8,0},{16,24},{24,16},{32,40},{40,32},{48,56},{56,48},{64,72... | collective-permute-start | bytes 1179656 | tf_op jit(solution)/shard_map/ppermute | solution.py:382
  62.7 17.7 %collective-permute-start.11 = (bf16[768,256]{1,0:T(8,128)(2,1)S(1)}, bf16[768,256]{1,0:T(8,128)(2,1)S(1)}, u32[]{:S(2)}, u32[]{:S(2)}) collective-permute-start(bf16[768,256]{1,0:T(8,128)(2,1)S(1)} %shard_map.139.refs_0_), channel_id=1, source_target_pairs={{0,32},{8,40},{16,48},{24,56},{32,64},{40,72},{48,80},{56,88},{64,... | collective-permute-start | bytes 1179656 | tf_op jit(solution)/shard_map/ppermute | solution.py:386
  80.4 12.7 %collective-permute-start.15 = (bf16[768,256]{1,0:T(8,128)(2,1)S(1)}, bf16[768,256]{1,0:T(8,128)(2,1)S(1)}, u32[]{:S(2)}, u32[]{:S(2)}) collective-permute-start(bf16[768,256]{1,0:T(8,128)(2,1)S(1)} %collective-permute-done.10.refs_4_), channel_id=1, source_target_pairs={{0,96},{8,104},{16,112},{24,120},{32,0},{40,8},{48,16},{56,24},{64... | collective-permute-start | bytes 1179656 | tf_op jit(solution)/shard_map/ppermute | solution.py:386
  80.4 12.7 %collective-permute-start.14 = (bf16[768,256]{1,0:T(8,128)(2,1)S(1)}, bf16[768,256]{1,0:T(8,128)(2,1)S(1)}, u32[]{:S(2)}, u32[]{:S(2)}) collective-permute-start(bf16[768,256]{1,0:T(8,128)(2,1)S(1)} %collective-permute-done.10.refs_4_), channel_id=1, source_target_pairs={{0,32},{8,40},{16,48},{24,56},{32,64},{40,72},{48,80},{56,88},{64,... | collective-permute-start | bytes 1179656 | tf_op jit(solution)/shard_map/ppermute | solution.py:386
  111.5 23.0 %collective-permute-start.25 = (bf16[96,4096]{1,0:T(8,128)(2,1)S(1)}, bf16[96,4096]{1,0:T(8,128)(2,1)S(1)}, u32[]{:S(2)}, u32[]{:S(2)}) collective-permute-start(bf16[96,4096]{1,0:T(8,128)(2,1)S(1)} %get-tuple-element.44), channel_id=1, source_target_pairs={{0,20},{1,21},{2,22},{3,23},{4,16},{5,17},{6,18},{7,19},{8,28},{9,... | collective-permute-start | bytes 2359304 | tf_op jit(solution)/shard_map/ppermute | solution.py:378
  111.9 22.9 %collective-permute-start.26 = (bf16[96,4096]{1,0:T(8,128)(2,1)S(1)}, bf16[96,4096]{1,0:T(8,128)(2,1)S(1)}, u32[]{:S(2)}, u32[]{:S(2)}) collective-permute-start(bf16[96,4096]{1,0:T(8,128)(2,1)S(1)} %get-tuple-element.46), channel_id=1, source_target_pairs={{0,1},{1,2},{2,3},{3,0},{4,5},{5,6},{6,7},{7,4},{8,9},{9,10},{10,1... | collective-permute-start | bytes 2359304 | tf_op jit(solution)/shard_map/ppermute | solution.py:371
  111.9 22.9 %collective-permute-start.27 = (bf16[96,4096]{1,0:T(8,128)(2,1)S(1)}, bf16[96,4096]{1,0:T(8,128)(2,1)S(1)}, u32[]{:S(2)}, u32[]{:S(2)}) collective-permute-start(bf16[96,4096]{1,0:T(8,128)(2,1)S(1)} %get-tuple-element.47), channel_id=1, source_target_pairs={{0,3},{1,0},{2,1},{3,2},{4,7},{5,4},{6,5},{7,6},{8,11},{9,8},{10,9... | collective-permute-start | bytes 2359304 | tf_op jit(solution)/shard_map/ppermute | solution.py:371
  135.1 12.7 %collective-permute-start.28 = (bf16[48,4096]{1,0:T(8,128)(2,1)S(1)}, bf16[48,4096]{1,0:T(8,128)(2,1)S(1)}, u32[]{:S(2)}, u32[]{:S(2)}) collective-permute-start(bf16[48,4096]{1,0:T(8,128)(2,1)S(1)} %get-tuple-element.55), channel_id=1, source_target_pairs={{0,1},{1,2},{2,3},{3,0},{4,5},{5,6},{6,7},{7,4},{8,9},{9,10},{10,1... | collective-permute-start | bytes 1179656 | tf_op jit(solution)/shard_map/ppermute | solution.py:371
  135.5 31.7 %collective-permute-start.32 = (bf16[48,4096]{1,0:T(8,128)(2,1)S(1)}, bf16[48,4096]{1,0:T(8,128)(2,1)S(1)}, u32[]{:S(2)}, u32[]{:S(2)}) collective-permute-start(bf16[48,4096]{1,0:T(8,128)(2,1)S(1)} %get-tuple-element.50), channel_id=1, source_target_pairs={{0,3},{1,0},{2,1},{3,2},{4,7},{5,4},{6,5},{7,6},{8,11},{9,8},{10,9... | collective-permute-start | bytes 1179656 | tf_op jit(solution)/shard_map/ppermute | solution.py:371
  138.7 28.5 %collective-permute-start.33 = (bf16[48,4096]{1,0:T(8,128)(2,1)S(1)}, bf16[48,4096]{1,0:T(8,128)(2,1)S(1)}, u32[]{:S(2)}, u32[]{:S(2)}) collective-permute-start(bf16[48,4096]{1,0:T(8,128)(2,1)S(1)} %get-tuple-element.51), channel_id=1, source_target_pairs={{0,1},{1,2},{2,3},{3,0},{4,5},{5,6},{6,7},{7,4},{8,9},{9,10},{10,1... | collective-permute-start | bytes 1179656 | tf_op jit(solution)/shard_map/ppermute | solution.py:371
  138.7 17.4 %collective-permute-start.30 = (bf16[48,4096]{1,0:T(8,128)(2,1)S(1)}, bf16[48,4096]{1,0:T(8,128)(2,1)S(1)}, u32[]{:S(2)}, u32[]{:S(2)}) collective-permute-start(bf16[48,4096]{1,0:T(8,128)(2,1)S(1)} %get-tuple-element.56), channel_id=1, source_target_pairs={{0,3},{1,0},{2,1},{3,2},{4,7},{5,4},{6,5},{7,6},{8,11},{9,8},{10,9... | collective-permute-start | bytes 1179656 | tf_op jit(solution)/shard_map/ppermute | solution.py:371
  141.9 25.3 %collective-permute-start.34 = (bf16[96,4096]{1,0:T(8,128)(2,1)S(1)}, bf16[96,4096]{1,0:T(8,128)(2,1)S(1)}, u32[]{:S(2)}, u32[]{:S(2)}) collective-permute-start(bf16[96,4096]{1,0:T(8,128)(2,1)S(1)} %add_convert_fusion.1), channel_id=1, source_target_pairs={{0,20},{1,21},{2,22},{3,23},{4,16},{5,17},{6,18},{7,19},{8,28},{9,... | collective-permute-start | bytes 2359304 | tf_op jit(solution)/shard_map/ppermute | solution.py:378
  147.9 19.3 %collective-permute-start.29 = (bf16[48,4096]{1,0:T(8,128)(2,1)S(1)}, bf16[48,4096]{1,0:T(8,128)(2,1)S(1)}, u32[]{:S(2)}, u32[]{:S(2)}) collective-permute-start(bf16[48,4096]{1,0:T(8,128)(2,1)S(1)} %add_convert_fusion.4), channel_id=1, source_target_pairs={{0,1},{1,2},{2,3},{3,0},{4,5},{5,6},{6,7},{7,4},{8,9},{9,10},{10,1... | collective-permute-start | bytes 1179656 | tf_op jit(solution)/shard_map/ppermute | solution.py:371
  156.2 12.9 %collective-permute-start.31 = (bf16[48,4096]{1,0:T(8,128)(2,1)S(1)}, bf16[48,4096]{1,0:T(8,128)(2,1)S(1)}, u32[]{:S(2)}, u32[]{:S(2)}) collective-permute-start(bf16[48,4096]{1,0:T(8,128)(2,1)S(1)} %add_convert_fusion.3), channel_id=1, source_target_pairs={{0,3},{1,0},{2,1},{3,2},{4,7},{5,4},{6,5},{7,6},{8,11},{9,8},{10,9... | collective-permute-start | bytes 1179656 | tf_op jit(solution)/shard_map/ppermute | solution.py:371
  (25 other events, 438.9 us)
where the time goes:
time: 173 us; the launch traced here: 170 us
  Pallas kernels  67 us (39%)
  waiting for transfers between devices  50 us (29%)
  starting transfers between devices  46.5 us (27%)
  other arithmetic  3.25 us (2%)
  local copies, waits for them, and re-layouts  3.23 us (2%)
    pallas_call x3, Pallas kernels, attend(): pl.pallas_call(functools.partial(attend_kernel, sections=sections, parts=...  33.1 us
    ppermute x16, waiting for transfers between devices, along_y(): lax.ppermute(rows, 'uly', [(z * 4 + y, z * 4 + (y + hop) % 4) for z in ra...  30.3 us
    ppermute x16, starting transfers between devices, along_y(): lax.ppermute(rows, 'uly', [(z * 4 + y, z * 4 + (y + hop) % 4) for z in ra...  27.1 us
    pallas_call x4, Pallas kernels, project(): pl.pallas_call(functools.partial(project_kernel, halves=halves, parts=len...  21.6 us
    ppermute x5, waiting for transfers between devices, along_x(): lax.ppermute(rows, 'blk', [(b, (b + 4 * hop) % 16) for b in range(16)])  12.4 us
    pallas_call x3, Pallas kernels, output(): pl.pallas_call(functools.partial(output_kernel, bases=bases), out_shape=t...  9.57 us
    ppermute x4, starting transfers between devices, across_z(): return lax.ppermute(rows, ('blk', 'uly'), pairs)  8.47 us
    ppermute x5, starting transfers between devices, along_x(): lax.ppermute(rows, 'blk', [(b, (b + 4 * hop) % 16) for b in range(16)])  7.95 us
  transfers between devices with their start and end apart: 35, of which 14 were waited for; matrix products, arithmetic and copies ran while one was open for 1% of the time, Pallas kernels for 25%

commit v1 on v0

--- a/solution.py
+++ b/solution.py
@@ -123,12 +123,12 @@
         out_shape=jax.ShapeDtypeStruct((count + sum(b.shape[0] for b in before), width), jnp.bfloat16),
         grid_spec=pltpu.PrefetchScalarGridSpec(
             num_scalar_prefetch=1,
-            grid=(depth // 1024,),
+            grid=(1,),
             in_specs=[HELD] * (len(rows) + len(before) + 1 + 2 * len(targets)),
             out_specs=HELD,
             scratch_shapes=[pltpu.VMEM((count, wide), jnp.float32)],
         ),
-        compiler_params=pltpu.CompilerParams(vmem_limit_bytes=14 * MIB),
+        compiler_params=pltpu.CompilerParams(vmem_limit_bytes=24 * MIB),
         cost_estimate=pl.CostEstimate(
             flops=4 * count * depth * wide,
             bytes_accessed=2 * depth * (wide + count),
@@ -312,7 +312,7 @@
 def output(info, mixed, weight, down, up, bases, halved):
     rows = sum(((PIECE // 2,) * 2 if b in halved else (PIECE,) for b in bases), ())
     features = weight.shape[1]
-    chunk = 1024
+    chunk = 4096
     depth = weight.shape[0] + up.shape[0]
     return pl.pallas_call(
         functools.partial(output_kernel, bases=bases),
@@ -324,7 +324,7 @@
             out_specs=(HELD,) * len(rows),
             scratch_shapes=[pltpu.VMEM((mixed.shape[0], depth), jnp.bfloat16)],
         ),
-        compiler_params=pltpu.CompilerParams(vmem_limit_bytes=12 * MIB),
+        compiler_params=pltpu.CompilerParams(vmem_limit_bytes=24 * MIB),
         cost_estimate=pl.CostEstimate(
             flops=2 * mixed.shape[0] * depth * features,
             bytes_accessed=2 * features * (depth + mixed.shape[0]),

time: 173 us -> 169 us (0.977)
  the two profiles are of different devices: /device:TPU:6 before, /device:TPU:60 now
where the time goes in v1:
time: 169 us
  waiting for transfers between devices  68.7 us (41%)
  Pallas kernels  61.4 us (36%)
  starting transfers between devices  32 us (19%)
  other arithmetic  3.25 us (2%)
  local copies, waits for them, and re-layouts  3.23 us (2%)
    ppermute x16, waiting for transfers between devices, along_y(): lax.ppermute(rows, 'uly', [(z * 4 + y, z * 4 + (y + hop) % 4) for z in ra...  42.3 us
    pallas_call x3, Pallas kernels, attend(): pl.pallas_call(functools.partial(attend_kernel, sections=sections, parts=...  33.1 us
    ppermute x16, starting transfers between devices, along_y(): lax.ppermute(rows, 'uly', [(z * 4 + y, z * 4 + (y + hop) % 4) for z in ra...  19.9 us
    pallas_call x4, Pallas kernels, project(): pl.pallas_call(functools.partial(project_kernel, halves=halves, parts=len...  18 us
    ppermute x5, waiting for transfers between devices, along_x(): lax.ppermute(rows, 'blk', [(b, (b + 4 * hop) % 16) for b in range(16)])  14.8 us
    pallas_call x3, Pallas kernels, output(): pl.pallas_call(functools.partial(output_kernel, bases=bases), out_shape=t...  7.51 us
    ppermute x10, waiting for transfers between devices, flipped(): return lax.ppermute(rows, 'blk', [(b, b ^ bit) for b in range(16)])  6.55 us
    ppermute x4, waiting for transfers between devices, across_z(): return lax.ppermute(rows, ('blk', 'uly'), pairs)  5.04 us
  transfers between devices with their start and end apart: 35, of which 16 were waited for; matrix products, arithmetic and copies ran while one was open for 1% of the time, Pallas kernels for 24%

profile of v1, /device:TPU:60, one launch (start us, length us, event | category | flops | bytes accessed | tf_op | source)
XLA Modules:
  0.0 168.9 jit_solution(6950878458229952629)
XLA Ops:
  0.0 2.8 %shard_map.136 = (bf16[96,4096]{1,0:T(8,128)(2,1)}, bf16[48,4096]{1,0:T(8,128)(2,1)}, bf16[48,4096]{1,0:T(8,128)(2,1)}) custom-call(bf16[96,4096]{1,0:T(8,128)(2,1)} %activations.1, f32[1,4096]{1,0:T(1,128)} %bitcast.20), custom_call_target="tpu_custom_call" | custom-call | tf_op jit(solution)/shard_map/pallas_call | solution.py:357
  6.8 8.8 %collective-permute-done.refs_1_ = bf16[48,4096]{1,0:T(8,128)(2,1)S(1)} collective-permute-done((bf16[48,4096]{1,0:T(8,128)(2,1)}, bf16[48,4096]{1,0:T(8,128)(2,1)S(1)}, u32[]{:S(2)}, u32[]{:S(2)}) %collective-permute-start) | collective-permute-done | bytes 393248 | tf_op jit(solution)/shard_map/ppermute | solution.py:371
  17.6 5.0 %collective-permute-done.4.refs_5_ = bf16[96,4096]{1,0:T(8,128)(2,1)} collective-permute-done((bf16[96,4096]{1,0:T(8,128)(2,1)}, bf16[96,4096]{1,0:T(8,128)(2,1)}, u32[]{:S(2)}, u32[]{:S(2)}) %collective-permute-start.4) | collective-permute-done | bytes 786464 | tf_op jit(solution)/shard_map/ppermute | solution.py:378
  25.8 4.1 %collective-permute-done.3.refs_4_ = bf16[48,4096]{1,0:T(8,128)(2,1)S(1)} collective-permute-done((bf16[48,4096]{1,0:T(8,128)(2,1)}, bf16[48,4096]{1,0:T(8,128)(2,1)S(1)}, u32[]{:S(2)}, u32[]{:S(2)}) %collective-permute-start.3) | collective-permute-done | bytes 393248 | tf_op jit(solution)/shard_map/ppermute | solution.py:371
  36.5 3.8 %shard_map.137.refs_5_ = bf16[384,256]{1,0:T(8,128)(2,1)S(1)} custom-call(s32[26]{0:T(128)S(1)} %concatenate.12.info, bf16[96,4096]{1,0:T(8,128)(2,1)S(1)} %copy-done.8, bf16[48,4096]{1,0:T(8,128)(2,1)S(1)} %collective-permute-done.refs_1_, bf16[48,4096]{1,0:T(8,128)(2,1)} %collective-permute-done.1.refs_2_, ...), custom_call_target="tpu_custom_call" | custom-call | flops 3221225472 | bytes 7340032 | tf_op jit(solution)/shard_map/pallas_call | solution.py:115
  40.2 5.0 %shard_map.138.q1 = bf16[384,512]{1,0:T(8,128)(2,1)S(1)} custom-call(s32[26]{0:T(128)S(1)} %concatenate.12.info, bf16[96,4096]{1,0:T(8,128)(2,1)S(1)} %copy-done.8, bf16[48,4096]{1,0:T(8,128)(2,1)S(1)} %collective-permute-done.refs_1_, bf16[48,4096]{1,0:T(8,128)(2,1)} %collective-permute-done.1.refs_2_, bf16[48,4096]{1,0:T(8,128)(2,1)S(1)} %collective-permute-done.2.refs_3_, ...), custom_call_target="tpu_custom_call" | custom-call | flops 4026531840 | bytes 8388608 | tf_op jit(solution)/shard_map/pallas_call | solution.py:115
  45.3 5.3 %collective-permute-done.5.refs_0_ = bf16[48,4096]{1,0:T(8,128)(2,1)S(1)} collective-permute-done((bf16[48,4096]{1,0:T(8,128)(2,1)}, bf16[48,4096]{1,0:T(8,128)(2,1)S(1)}, u32[]{:S(2)}, u32[]{:S(2)}) %collective-permute-start.5) | collective-permute-done | bytes 393248 | tf_op jit(solution)/shard_map/ppermute | solution.py:371
  50.6 2.6 %collective-permute-done.6.refs_1_ = bf16[48,4096]{1,0:T(8,128)(2,1)S(1)} collective-permute-done((bf16[48,4096]{1,0:T(8,128)(2,1)}, bf16[48,4096]{1,0:T(8,128)(2,1)S(1)}, u32[]{:S(2)}, u32[]{:S(2)}) %collective-permute-start.6) | collective-permute-done | bytes 393248 | tf_op jit(solution)/shard_map/ppermute | solution.py:371
  53.2 4.1 %shard_map.139.refs_0_ = bf16[768,256]{1,0:T(8,128)(2,1)S(1)} custom-call(s32[26]{0:T(128)S(1)} %concatenate.12.info, bf16[48,4096]{1,0:T(8,128)(2,1)S(1)} %collective-permute-done.5.refs_0_, bf16[48,4096]{1,0:T(8,128)(2,1)S(1)} %collective-permute-done.6.refs_1_, bf16[96,4096]{1,0:T(8,128)(2,1)} %collective-permute-done.7.refs_2_, ...), custom_call_target="tpu_custom_call" | custom-call | flops 3221225472 | bytes 7340032 | tf_op jit(solution)/shard_map/pallas_call | solution.py:115
  62.4 5.1 %shard_map.140.q2 = bf16[384,512]{1,0:T(8,128)(2,1)S(1)} custom-call(s32[26]{0:T(128)S(1)} %concatenate.12.info, bf16[48,4096]{1,0:T(8,128)(2,1)S(1)} %collective-permute-done.5.refs_0_, bf16[48,4096]{1,0:T(8,128)(2,1)S(1)} %collective-permute-done.6.refs_1_, bf16[96,4096]{1,0:T(8,128)(2,1)} %collective-permute-done.7.refs_2_, ...), custom_call_target="tpu_custom_call" | custom-call | flops 4026531840 | bytes 8388608 | tf_op jit(solution)/shard_map/pallas_call | solution.py:115
  67.6 5.7 %collective-permute-done.13.refs_3_ = bf16[768,256]{1,0:T(8,128)(2,1)S(1)} collective-permute-done((bf16[768,256]{1,0:T(8,128)(2,1)S(1)}, bf16[768,256]{1,0:T(8,128)(2,1)S(1)}, u32[]{:S(2)}, u32[]{:S(2)}) %collective-permute-start.13) | collective-permute-done | bytes 393248 | tf_op jit(solution)/shard_map/ppermute | solution.py:386
  73.5 4.2 %collective-permute-done.12.refs_2_ = bf16[768,256]{1,0:T(8,128)(2,1)S(1)} collective-permute-done((bf16[768,256]{1,0:T(8,128)(2,1)S(1)}, bf16[768,256]{1,0:T(8,128)(2,1)S(1)}, u32[]{:S(2)}, u32[]{:S(2)}) %collective-permute-start.12) | collective-permute-done | bytes 393248 | tf_op jit(solution)/shard_map/ppermute | solution.py:386
  80.0 4.8 %collective-permute-done.16.refs_7_ = bf16[768,256]{1,0:T(8,128)(2,1)S(1)} collective-permute-done((bf16[768,256]{1,0:T(8,128)(2,1)S(1)}, bf16[768,256]{1,0:T(8,128)(2,1)S(1)}, u32[]{:S(2)}, u32[]{:S(2)}) %collective-permute-start.16) | collective-permute-done | bytes 393248 | tf_op jit(solution)/shard_map/ppermute | solution.py:382
  85.4 4.1 %collective-permute-done.15.refs_6_ = bf16[768,256]{1,0:T(8,128)(2,1)S(1)} collective-permute-done((bf16[768,256]{1,0:T(8,128)(2,1)S(1)}, bf16[768,256]{1,0:T(8,128)(2,1)S(1)}, u32[]{:S(2)}, u32[]{:S(2)}) %collective-permute-start.15) | collective-permute-done | bytes 393248 | tf_op jit(solution)/shard_map/ppermute | solution.py:386
  92.0 10.7 %shard_map.141 = (bf16[288,512]{1,0:T(8,128)(2,1)S(1)}, bf16[16,768,256]{2,1,0:T(8,128)(2,1)S(1)}) custom-call(s32[26]{0:T(128)S(1)} %concatenate.12.info, bf16[384,512]{1,0:T(8,128)(2,1)S(1)} %shard_map.138.q1, bf16[384,512]{1,0:T(8,128)(2,1)S(1)} %shard_map.140.q2, bf16[768,256]{1,0:T(8,128)(2,1)S(1)} %shard_map.139.refs_0_, ...), custom_call_target="tpu_custom_call" | custom-call | flops 7247757312 | bytes 8388608 | tf_op jit(solution)/shard_map/pallas_call | solution.py:266
  102.8 2.6 %shard_map.144 = (bf16[96,4096]{1,0:T(8,128)(2,1)S(1)}, bf16[96,4096]{1,0:T(8,128)(2,1)S(1)}, bf16[96,4096]{1,0:T(8,128)(2,1)S(1)}) custom-call(s32[26]{0:T(128)S(1)} %concatenate.12.info, bf16[288,512]{1,0:T(8,128)(2,1)S(1)} %get-tuple-element.43.mixed, bf16[512,4096]{1,0:T(8,128)(2,1)S(1)} %copy-done, bf16[512,128]{1,0:T(8,128)(2,1)S(1)} %copy-done.2, ...), custom_call_target="tpu_custom_call" | custom-call | flops 1509949440 | bytes 7602176 | tf_op jit(solution)/shard_map/pallas_call | solution.py:317
  110.1 16.5 %shard_map.142.mixed = bf16[384,512]{1,0:T(8,128)(2,1)S(1)} custom-call(s32[26]{0:T(128)S(1)} %concatenate.12.info, bf16[384,512]{1,0:T(8,128)(2,1)S(1)} %shard_map.138.q1, bf16[384,512]{1,0:T(8,128)(2,1)S(1)} %shard_map.140.q2, bf16[16,768,256]{2,1,0:T(8,128)(2,1)S(1)} %get-tuple-element.40.refs_0_), custom_call_target="tpu_custom_call" | custom-call | flops 9663676416 | bytes 8388608 | tf_op jit(solution)/shard_map/pallas_call | solution.py:266
  126.6 3.3 %shard_map.143 = (bf16[96,4096]{1,0:T(8,128)(2,1)S(1)}, bf16[48,4096]{1,0:T(8,128)(2,1)S(1)}, bf16[48,4096]{1,0:T(8,128)(2,1)S(1)}, bf16[48,4096]{1,0:T(8,128)(2...) custom-call(s32[26]{0:T(128)S(1)} %concatenate.12.info, bf16[384,512]{1,0:T(8,128)(2,1)S(1)} %shard_map.142.mixed, ...), custom_call_target="tpu_custom_call" | custom-call | flops 2013265920 | bytes 8388608 | tf_op jit(solution)/shard_map/pallas_call | solution.py:317
  133.7 3.2 %collective-permute-start.33 = (bf16[48,4096]{1,0:T(8,128)(2,1)S(1)}, bf16[48,4096]{1,0:T(8,128)(2,1)S(1)}, u32[]{:S(2)}, u32[]{:S(2)}) collective-permute-start(bf16[48,4096]{1,0:T(8,128)(2,1)S(1)} %get-tuple-element.51), channel_id=1, source_target_pairs={{0,1},{1,2},{2,3},{3,0},{4,5},{5,6},{6,7},{7,4},{8,9},{9,10},{10,1... | collective-permute-start | bytes 1179656 | tf_op jit(solution)/shard_map/ppermute | solution.py:371
  137.0 6.7 %collective-permute-done.28 = bf16[48,4096]{1,0:T(8,128)(2,1)S(1)} collective-permute-done((bf16[48,4096]{1,0:T(8,128)(2,1)S(1)}, bf16[48,4096]{1,0:T(8,128)(2,1)S(1)}, u32[]{:S(2)}, u32[]{:S(2)}) %collective-permute-start.28) | collective-permute-done | bytes 393248 | tf_op jit(solution)/shard_map/ppermute | solution.py:371
  143.8 2.6 %collective-permute-start.29 = (bf16[48,4096]{1,0:T(8,128)(2,1)S(1)}, bf16[48,4096]{1,0:T(8,128)(2,1)S(1)}, u32[]{:S(2)}, u32[]{:S(2)}) collective-permute-start(bf16[48,4096]{1,0:T(8,128)(2,1)S(1)} %add_convert_fusion.4), channel_id=1, source_target_pairs={{0,1},{1,2},{2,3},{3,0},{4,5},{5,6},{6,7},{7,4},{8,9},{9,10},{10,1... | collective-permute-start | bytes 1179656 | tf_op jit(solution)/shard_map/ppermute | solution.py:371
  146.4 8.6 %collective-permute-done.30 = bf16[48,4096]{1,0:T(8,128)(2,1)S(1)} collective-permute-done((bf16[48,4096]{1,0:T(8,128)(2,1)S(1)}, bf16[48,4096]{1,0:T(8,128)(2,1)S(1)}, u32[]{:S(2)}, u32[]{:S(2)}) %collective-permute-start.30) | collective-permute-done | bytes 393248 | tf_op jit(solution)/shard_map/ppermute | solution.py:371
  155.1 5.8 %shard_map.145.mixed = bf16[96,512]{1,0:T(8,128)(2,1)S(1)} custom-call(s32[26]{0:T(128)S(1)} %concatenate.12.info, bf16[384,512]{1,0:T(8,128)(2,1)S(1)} %shard_map.138.q1, bf16[384,512]{1,0:T(8,128)(2,1)S(1)} %shard_map.140.q2, bf16[16,768,256]{2,1,0:T(8,128)(2,1)S(1)} %get-tuple-element.40.refs_0_), custom_call_target="tpu_custom_call" | custom-call | flops 2415919104 | bytes 8388608 | tf_op jit(solution)/shard_map/pallas_call | solution.py:266
  162.6 4.9 %collective-permute-done.31 = bf16[48,4096]{1,0:T(8,128)(2,1)S(1)} collective-permute-done((bf16[48,4096]{1,0:T(8,128)(2,1)S(1)}, bf16[48,4096]{1,0:T(8,128)(2,1)S(1)}, u32[]{:S(2)}, u32[]{:S(2)}) %collective-permute-start.31) | collective-permute-done | bytes 393248 | tf_op jit(solution)/shard_map/ppermute | solution.py:371
  (95 shorter events, 38.1 us)
Async XLA Ops:
  2.8 19.8 %collective-permute-start.4 = (bf16[96,4096]{1,0:T(8,128)(2,1)}, bf16[96,4096]{1,0:T(8,128)(2,1)}, u32[]{:S(2)}, u32[]{:S(2)}) collective-permute-start(bf16[96,4096]{1,0:T(8,128)(2,1)} %get-tuple-element.30.refs_0_), channel_id=1, source_target_pairs={{0,20},{1,21},{2,22},{3,23},{4,16},{5,17},{6,18},{7,19},{8,28},{9,... | collective-permute-start | bytes 2359304 | tf_op jit(solution)/shard_map/ppermute | solution.py:378
  5.0 12.1 %collective-permute-start.1 = (bf16[48,4096]{1,0:T(8,128)(2,1)}, bf16[48,4096]{1,0:T(8,128)(2,1)}, u32[]{:S(2)}, u32[]{:S(2)}) collective-permute-start(bf16[48,4096]{1,0:T(8,128)(2,1)} %get-tuple-element.35), channel_id=1, source_target_pairs={{0,3},{1,0},{2,1},{3,2},{4,7},{5,4},{6,5},{7,6},{8,11},{9,8},{10,9... | collective-permute-start | bytes 1179656 | tf_op jit(solution)/shard_map/ppermute | solution.py:371
  17.0 12.9 %collective-permute-start.3 = (bf16[48,4096]{1,0:T(8,128)(2,1)}, bf16[48,4096]{1,0:T(8,128)(2,1)S(1)}, u32[]{:S(2)}, u32[]{:S(2)}) collective-permute-start(bf16[48,4096]{1,0:T(8,128)(2,1)} %collective-permute-done.1.refs_2_), channel_id=1, source_target_pairs={{0,3},{1,0},{2,1},{3,2},{4,7},{5,4},{6,5},{7,6},{8,11},{9,8},{10,9... | collective-permute-start | bytes 1179656 | tf_op jit(solution)/shard_map/ppermute | solution.py:371
  22.6 30.6 %collective-permute-start.8 = (bf16[96,4096]{1,0:T(8,128)(2,1)}, bf16[96,4096]{1,0:T(8,128)(2,1)}, u32[]{:S(2)}, u32[]{:S(2)}) collective-permute-start(bf16[96,4096]{1,0:T(8,128)(2,1)} %collective-permute-done.4.refs_5_), channel_id=1, source_target_pairs={{0,3},{1,0},{2,1},{3,2},{4,7},{5,4},{6,5},{7,6},{8,11},{9,8},{10,9... | collective-permute-start | bytes 2359304 | tf_op jit(solution)/shard_map/ppermute | solution.py:371
  23.3 29.8 %collective-permute-start.7 = (bf16[96,4096]{1,0:T(8,128)(2,1)}, bf16[96,4096]{1,0:T(8,128)(2,1)}, u32[]{:S(2)}, u32[]{:S(2)}) collective-permute-start(bf16[96,4096]{1,0:T(8,128)(2,1)} %collective-permute-done.4.refs_5_), channel_id=1, source_target_pairs={{0,1},{1,2},{2,3},{3,0},{4,5},{5,6},{6,7},{7,4},{8,9},{9,10},{10,1... | collective-permute-start | bytes 2359304 | tf_op jit(solution)/shard_map/ppermute | solution.py:371
  30.9 22.3 %collective-permute-start.9 = (bf16[96,4096]{1,0:T(8,128)(2,1)}, bf16[96,4096]{1,0:T(8,128)(2,1)}, u32[]{:S(2)}, u32[]{:S(2)}) collective-permute-start(bf16[96,4096]{1,0:T(8,128)(2,1)} %pad_maximum_fusion), channel_id=1, source_target_pairs={{0,20},{1,21},{2,22},{3,23},{4,16},{5,17},{6,18},{7,19},{8,28},{9,... | collective-permute-start | bytes 2359304 | tf_op jit(solution)/shard_map/ppermute | solution.py:378
  31.3 19.3 %collective-permute-start.5 = (bf16[48,4096]{1,0:T(8,128)(2,1)}, bf16[48,4096]{1,0:T(8,128)(2,1)S(1)}, u32[]{:S(2)}, u32[]{:S(2)}) collective-permute-start(bf16[48,4096]{1,0:T(8,128)(2,1)} %get-tuple-element.35), channel_id=1, source_target_pairs={{0,1},{1,2},{2,3},{3,0},{4,5},{5,6},{6,7},{7,4},{8,9},{9,10},{10,1... | collective-permute-start | bytes 1179656 | tf_op jit(solution)/shard_map/ppermute | solution.py:371
  31.4 21.8 %collective-permute-start.6 = (bf16[48,4096]{1,0:T(8,128)(2,1)}, bf16[48,4096]{1,0:T(8,128)(2,1)S(1)}, u32[]{:S(2)}, u32[]{:S(2)}) collective-permute-start(bf16[48,4096]{1,0:T(8,128)(2,1)} %get-tuple-element.36), channel_id=1, source_target_pairs={{0,3},{1,0},{2,1},{3,2},{4,7},{5,4},{6,5},{7,6},{8,11},{9,8},{10,9... | collective-permute-start | bytes 1179656 | tf_op jit(solution)/shard_map/ppermute | solution.py:371
  59.8 13.6 %collective-permute-start.13 = (bf16[768,256]{1,0:T(8,128)(2,1)S(1)}, bf16[768,256]{1,0:T(8,128)(2,1)S(1)}, u32[]{:S(2)}, u32[]{:S(2)}) collective-permute-start(bf16[768,256]{1,0:T(8,128)(2,1)S(1)} %shard_map.139.refs_0_), channel_id=1, source_target_pairs={{0,64},{8,72},{16,80},{24,88},{32,96},{40,104},{48,112},{56,120},{... | collective-permute-start | bytes 1179656 | tf_op jit(solution)/shard_map/ppermute | solution.py:386
  60.3 17.3 %collective-permute-start.12 = (bf16[768,256]{1,0:T(8,128)(2,1)S(1)}, bf16[768,256]{1,0:T(8,128)(2,1)S(1)}, u32[]{:S(2)}, u32[]{:S(2)}) collective-permute-start(bf16[768,256]{1,0:T(8,128)(2,1)S(1)} %shard_map.139.refs_0_), channel_id=1, source_target_pairs={{0,96},{8,104},{16,112},{24,120},{32,0},{40,8},{48,16},{56,24},{64... | collective-permute-start | bytes 1179656 | tf_op jit(solution)/shard_map/ppermute | solution.py:386
  62.4 15.2 %collective-permute-start.17 = (bf16[768,256]{1,0:T(8,128)(2,1)S(1)}, bf16[768,256]{1,0:T(8,128)(2,1)S(1)}, u32[]{:S(2)}, u32[]{:S(2)}) collective-permute-start(bf16[768,256]{1,0:T(8,128)(2,1)S(1)} %shard_map.139.refs_0_), channel_id=1, source_target_pairs={{0,8},{8,0},{16,24},{24,16},{32,40},{40,32},{48,56},{56,48},{64,72... | collective-permute-start | bytes 1179656 | tf_op jit(solution)/shard_map/ppermute | solution.py:382
  62.4 16.6 %collective-permute-start.11 = (bf16[768,256]{1,0:T(8,128)(2,1)S(1)}, bf16[768,256]{1,0:T(8,128)(2,1)S(1)}, u32[]{:S(2)}, u32[]{:S(2)}) collective-permute-start(bf16[768,256]{1,0:T(8,128)(2,1)S(1)} %shard_map.139.refs_0_), channel_id=1, source_target_pairs={{0,32},{8,40},{16,48},{24,56},{32,64},{40,72},{48,80},{56,88},{64,... | collective-permute-start | bytes 1179656 | tf_op jit(solution)/shard_map/ppermute | solution.py:386
  73.3 11.5 %collective-permute-start.16 = (bf16[768,256]{1,0:T(8,128)(2,1)S(1)}, bf16[768,256]{1,0:T(8,128)(2,1)S(1)}, u32[]{:S(2)}, u32[]{:S(2)}) collective-permute-start(bf16[768,256]{1,0:T(8,128)(2,1)S(1)} %collective-permute-done.13.refs_3_), channel_id=1, source_target_pairs={{0,16},{8,24},{16,0},{24,8},{32,48},{40,56},{48,32},{56,40},{64,80... | collective-permute-start | bytes 1179656 | tf_op jit(solution)/shard_map/ppermute | solution.py:382
  77.6 11.9 %collective-permute-start.15 = (bf16[768,256]{1,0:T(8,128)(2,1)S(1)}, bf16[768,256]{1,0:T(8,128)(2,1)S(1)}, u32[]{:S(2)}, u32[]{:S(2)}) collective-permute-start(bf16[768,256]{1,0:T(8,128)(2,1)S(1)} %collective-permute-done.10.refs_4_), channel_id=1, source_target_pairs={{0,96},{8,104},{16,112},{24,120},{32,0},{40,8},{48,16},{56,24},{64... | collective-permute-start | bytes 1179656 | tf_op jit(solution)/shard_map/ppermute | solution.py:386
  105.4 24.4 %collective-permute-start.25 = (bf16[96,4096]{1,0:T(8,128)(2,1)S(1)}, bf16[96,4096]{1,0:T(8,128)(2,1)S(1)}, u32[]{:S(2)}, u32[]{:S(2)}) collective-permute-start(bf16[96,4096]{1,0:T(8,128)(2,1)S(1)} %get-tuple-element.44), channel_id=1, source_target_pairs={{0,20},{1,21},{2,22},{3,23},{4,16},{5,17},{6,18},{7,19},{8,28},{9,... | collective-permute-start | bytes 2359304 | tf_op jit(solution)/shard_map/ppermute | solution.py:378
  107.5 22.5 %collective-permute-start.26 = (bf16[96,4096]{1,0:T(8,128)(2,1)S(1)}, bf16[96,4096]{1,0:T(8,128)(2,1)S(1)}, u32[]{:S(2)}, u32[]{:S(2)}) collective-permute-start(bf16[96,4096]{1,0:T(8,128)(2,1)S(1)} %get-tuple-element.46), channel_id=1, source_target_pairs={{0,1},{1,2},{2,3},{3,0},{4,5},{5,6},{6,7},{7,4},{8,9},{9,10},{10,1... | collective-permute-start | bytes 2359304 | tf_op jit(solution)/shard_map/ppermute | solution.py:371
  110.1 21.2 %collective-permute-start.27 = (bf16[96,4096]{1,0:T(8,128)(2,1)S(1)}, bf16[96,4096]{1,0:T(8,128)(2,1)S(1)}, u32[]{:S(2)}, u32[]{:S(2)}) collective-permute-start(bf16[96,4096]{1,0:T(8,128)(2,1)S(1)} %get-tuple-element.47), channel_id=1, source_target_pairs={{0,3},{1,0},{2,1},{3,2},{4,7},{5,4},{6,5},{7,6},{8,11},{9,8},{10,9... | collective-permute-start | bytes 2359304 | tf_op jit(solution)/shard_map/ppermute | solution.py:371
  131.6 12.1 %collective-permute-start.28 = (bf16[48,4096]{1,0:T(8,128)(2,1)S(1)}, bf16[48,4096]{1,0:T(8,128)(2,1)S(1)}, u32[]{:S(2)}, u32[]{:S(2)}) collective-permute-start(bf16[48,4096]{1,0:T(8,128)(2,1)S(1)} %get-tuple-element.55), channel_id=1, source_target_pairs={{0,1},{1,2},{2,3},{3,0},{4,5},{5,6},{6,7},{7,4},{8,9},{9,10},{10,1... | collective-permute-start | bytes 1179656 | tf_op jit(solution)/shard_map/ppermute | solution.py:371
  133.7 28.9 %collective-permute-start.32 = (bf16[48,4096]{1,0:T(8,128)(2,1)S(1)}, bf16[48,4096]{1,0:T(8,128)(2,1)S(1)}, u32[]{:S(2)}, u32[]{:S(2)}) collective-permute-start(bf16[48,4096]{1,0:T(8,128)(2,1)S(1)} %get-tuple-element.50), channel_id=1, source_target_pairs={{0,3},{1,0},{2,1},{3,2},{4,7},{5,4},{6,5},{7,6},{8,11},{9,8},{10,9... | collective-permute-start | bytes 1179656 | tf_op jit(solution)/shard_map/ppermute | solution.py:371
  133.7 28.9 %collective-permute-start.33 = (bf16[48,4096]{1,0:T(8,128)(2,1)S(1)}, bf16[48,4096]{1,0:T(8,128)(2,1)S(1)}, u32[]{:S(2)}, u32[]{:S(2)}) collective-permute-start(bf16[48,4096]{1,0:T(8,128)(2,1)S(1)} %get-tuple-element.51), channel_id=1, source_target_pairs={{0,1},{1,2},{2,3},{3,0},{4,5},{5,6},{6,7},{7,4},{8,9},{9,10},{10,1... | collective-permute-start | bytes 1179656 | tf_op jit(solution)/shard_map/ppermute | solution.py:371
  137.0 18.0 %collective-permute-start.30 = (bf16[48,4096]{1,0:T(8,128)(2,1)S(1)}, bf16[48,4096]{1,0:T(8,128)(2,1)S(1)}, u32[]{:S(2)}, u32[]{:S(2)}) collective-permute-start(bf16[48,4096]{1,0:T(8,128)(2,1)S(1)} %get-tuple-element.56), channel_id=1, source_target_pairs={{0,3},{1,0},{2,1},{3,2},{4,7},{5,4},{6,5},{7,6},{8,11},{9,8},{10,9... | collective-permute-start | bytes 1179656 | tf_op jit(solution)/shard_map/ppermute | solution.py:371
  137.0 25.7 %collective-permute-start.34 = (bf16[96,4096]{1,0:T(8,128)(2,1)S(1)}, bf16[96,4096]{1,0:T(8,128)(2,1)S(1)}, u32[]{:S(2)}, u32[]{:S(2)}) collective-permute-start(bf16[96,4096]{1,0:T(8,128)(2,1)S(1)} %add_convert_fusion.1), channel_id=1, source_target_pairs={{0,20},{1,21},{2,22},{3,23},{4,16},{5,17},{6,18},{7,19},{8,28},{9,... | collective-permute-start | bytes 2359304 | tf_op jit(solution)/shard_map/ppermute | solution.py:378
  143.8 18.8 %collective-permute-start.29 = (bf16[48,4096]{1,0:T(8,128)(2,1)S(1)}, bf16[48,4096]{1,0:T(8,128)(2,1)S(1)}, u32[]{:S(2)}, u32[]{:S(2)}) collective-permute-start(bf16[48,4096]{1,0:T(8,128)(2,1)S(1)} %add_convert_fusion.4), channel_id=1, source_target_pairs={{0,1},{1,2},{2,3},{3,0},{4,5},{5,6},{6,7},{7,4},{8,9},{9,10},{10,1... | collective-permute-start | bytes 1179656 | tf_op jit(solution)/shard_map/ppermute | solution.py:371
  155.0 12.5 %collective-permute-start.31 = (bf16[48,4096]{1,0:T(8,128)(2,1)S(1)}, bf16[48,4096]{1,0:T(8,128)(2,1)S(1)}, u32[]{:S(2)}, u32[]{:S(2)}) collective-permute-start(bf16[48,4096]{1,0:T(8,128)(2,1)S(1)} %add_convert_fusion.3), channel_id=1, source_target_pairs={{0,3},{1,0},{2,1},{3,2},{4,7},{5,4},{6,5},{7,6},{8,11},{9,8},{10,9... | collective-permute-start | bytes 1179656 | tf_op jit(solution)/shard_map/ppermute | solution.py:371
  (25 other events, 411.2 us)
